TPU v7x, 512 devices: a whole 4x4x16 slice. The times are simulated.
512 devices in a mesh: dp: 32 (over y, x, core), tensor: 16 (over z).
Axes of the slice: x: 4, y: 4, z: 16, core: 2. Of those that a mesh axis runs over, the one named last changes fastest.
Arguments:
- rows_in: bfloat16 [16384, 8192], P('dp', 'tensor'), may hold values from -6 to 6
- adapter_ids: int32 [16384], P('dp'), may hold values from 0 to 511, as said below
- row_counts: int32 [32], P('dp'), may hold values from 256 to 512, as said below
- adapter_slot: int32 [512], replicated, may hold values from 0 to 511, each once
- adapter_a: bfloat16 [512, 16, 16], P(('dp', 'tensor')), may hold values from -1.5 to 1.5
- adapter_b: bfloat16 [512, 512, 1792], P(('dp', 'tensor')), may hold values from -0.25 to 0.25
Outputs:
- delta: bfloat16 [16384, 28672], P('dp', 'tensor')
Inputs may be any that keep to these rules, and one draw needn't show every extreme that they name: `adapter_ids`: within the 512 rows of one dp group (live or not), every adapter that is named is named by exactly 2 rows; some adapter is named by 2 live rows in every group. The live rows of a group are its first row_counts rows; some group has all 512 rows live. `adapter_slot`: each storage index appears once; storage index s is held by the device whose flattened dp, tensor index is s.
All inputs are finite; a program needn't handle non-finite values.
Results may differ from a plain program's by a relative error of at most 0.0049.
Values may be sent and summed in bfloat16 or wider, within the bound.
A program may use at most 128 MiB of HBM per device.

v0:
```python
import jax
import jax.numpy as jnp
from jax import lax
from jax.sharding import PartitionSpec as P

FA = 16
BIN = 512
BOUT = 1792


def on_device(rows_in, adapter_ids, row_counts, adapter_slot, adapter_a, adapter_b):
    group_count = lax.axis_size("dp")
    tensor_count = lax.axis_size("tensor")
    owner_count = group_count * tensor_count
    group_rows, feature_cols = rows_in.shape
    cap = max(2, group_rows // owner_count)
    catalog = jnp.arange(adapter_slot.shape[0], dtype=jnp.int32)
    id_match = adapter_ids[:, None] == catalog[None, :]
    owner_dev = jnp.sum(jnp.where(id_match, adapter_slot[None, :], 0), axis=1)
    position = jnp.arange(group_rows, dtype=jnp.int32)
    row_live = position < row_counts[0]
    earlier_same = (
        (owner_dev[:, None] == owner_dev[None, :])
        & (position[None, :] < position[:, None])
        & row_live[None, :]
    )
    slot_rank = jnp.sum(earlier_same.astype(jnp.int32), axis=1)
    slot_index = owner_dev * cap + slot_rank
    target = jnp.where(row_live, slot_index, owner_count * cap)
    buffer = (
        jnp.zeros((owner_count * cap, feature_cols), jnp.bfloat16)
        .at[target]
        .set(rows_in, mode="drop")
    )
    buffer = buffer.reshape(group_count, tensor_count, cap, feature_cols)
    arrived = lax.all_to_all(
        lax.all_to_all(buffer, "dp", split_axis=0, concat_axis=0, tiled=True),
        "tensor",
        split_axis=1,
        concat_axis=3,
        tiled=True,
    )
    whole_rows = arrived.reshape(group_count * cap, FA, BIN)
    mixed = jnp.einsum(
        "rij,ik->rkj", whole_rows, adapter_a[0], preferred_element_type=jnp.float32
    ).astype(jnp.bfloat16)
    result = jnp.dot(
        mixed.reshape(group_count * cap * FA, BIN), adapter_b[0], preferred_element_type=jnp.float32
    )
    result = result.astype(jnp.bfloat16).reshape(group_count, 1, cap, FA * BOUT)
    split_back = lax.all_to_all(result, "tensor", split_axis=3, concat_axis=1, tiled=True)
    returned = lax.all_to_all(split_back, "dp", split_axis=0, concat_axis=0, tiled=True)
    returned = returned.reshape(owner_count * cap, returned.shape[3])
    picked = jnp.take(returned, jnp.where(row_live, slot_index, 0), axis=0)
    return jnp.where(row_live[:, None], picked, jnp.zeros_like(picked))


def solution(mesh):
    return jax.shard_map(
        on_device,
        mesh=mesh,
        in_specs=(
            P("dp", "tensor"),
            P("dp"),
            P("dp"),
            P(),
            P(("dp", "tensor"), None, None),
            P(("dp", "tensor"), None, None),
        ),
        out_specs=P("dp", "tensor"),
        check_vma=False,
    )
```

profile of v0, /device:TPU:32, one launch (start us, length us, event | category | flops | bytes accessed | tf_op | source)
XLA Modules:
  0.0 458.7 jit_solution(2098749917473446583)
XLA Ops:
  0.0 0.0 copy-start
  0.8 0.9 select_reduce_fusion
  1.7 0.3 convert_reduce_fusion
  2.1 3.2 scatter_custom_fusion
  5.3 1.2 reshape.90
  6.5 24.7 %all_to_all.43 = bf16[32,16,2,512]{3,2,1,0:T(2,128)(2,1)S(1)} all-to-all(bf16[32,16,2,512]{3,2,1,0:T(2,128)(2,1)} %reshape.90), channel_id=1, replica_groups=mesh['dp'=32,'tensor'=16] {'dp'}, dimensions={0} | all-to-all | bytes 2097152 | tf_op jit(solution)/shard_map/all_to_all | solution.py:37
  31.2 1.0 copy.22
  32.1 0.0 copy-start.2
  32.1 66.4 %all_to_all.44 = bf16[32,16,2,512]{3,2,0,1:T(2,128)(2,1)S(1)} all-to-all(bf16[32,16,2,512]{3,2,0,1:T(2,128)(2,1)S(1)} %copy.22), channel_id=1, replica_groups=mesh['dp'=32,'tensor'=16] {'tensor'}, dimensions={1} | all-to-all | bytes 2097152 | tf_op jit(solution)/shard_map/all_to_all | solution.py:36
  98.5 0.9 copy.23
  99.4 0.0 copy-done.2
  99.4 0.5 convolution_convert_fusion.1
  99.8 0.0 copy-done
  99.9 3.9 convolution_convert_fusion
  103.7 8.4 %reshape.93 = bf16[32,1,2,28672]{3,2,0,1:T(2,128)(2,1)} reshape(bf16[1024,1792]{1,0:T(8,128)(2,1)} %convolution_convert_fusion) | data formatting | bytes 7340032 | tf_op jit(solution)/shard_map/reshape | solution.py:50
  112.1 34.8 %copy.25 = bf16[32,1,2,28672]{0,2,1,3:T(2,128)(2,1)} copy(bf16[32,1,2,28672]{3,2,0,1:T(2,128)(2,1)} %reshape.93) | data formatting | bytes 7340032 | tf_op jit(solution)/shard_map/reshape | solution.py:50
  147.0 19.3 %reshape.114 = bf16[16,2,57344]{2,1,0:T(2,128)(2,1)} reshape(bf16[28672,1,2,32]{3,2,1,0:T(2,128)(2,1)} %bitcast.30) | data formatting | bytes 7340032
  166.3 170.2 %all_to_all.45 = bf16[16,2,57344]{2,1,0:T(2,128)(2,1)} all-to-all(bf16[16,2,57344]{2,1,0:T(2,128)(2,1)} %reshape.114), channel_id=1, replica_groups=mesh['dp'=32,'tensor'=16] {'tensor'}, dimensions={0} | all-to-all | bytes 7340032 | tf_op jit(solution)/shard_map/all_to_all | solution.py:51
  336.5 15.6 %reshape.115 = bf16[28672,1,2,32]{3,2,1,0:T(2,128)(2,1)} reshape(bf16[16,2,57344]{2,1,0:T(2,128)(2,1)} %all_to_all.45) | data formatting | bytes 7340032
  352.1 35.1 %copy.26 = bf16[32,1,2,16,1792]{4,2,3,0,1:T(2,128)(2,1)} copy(bf16[32,1,2,16,1792]{0,2,4,3,1:T(2,128)(2,1)} %bitcast.31) | data formatting | bytes 7340032 | tf_op jit(solution)/shard_map/all_to_all | solution.py:51
  387.1 5.0 %all-to-all-start.3 = ((bf16[32,16,2,1792]{3,2,1,0:T(2,128)(2,1)}), bf16[32,16,2,1792]{3,2,1,0:T(2,128)(2,1)}, u32[]{:S(2)}, u32[]{:S(2)}) async-start(bf16[32,16,2,1792]{3,2,1,0:T(2,128)(2,1)} %bitcast.32), calls=%async_computation.3 | async-start | bytes 7340032 | tf_op jit(solution)/shard_map/all_to_all | solution.py:52
  392.2 47.5 %all-to-all-done.3 = bf16[32,16,2,1792]{3,2,1,0:T(2,128)(2,1)} async-done(((bf16[32,16,2,1792]{3,2,1,0:T(2,128)(2,1)}), bf16[32,16,2,1792]{3,2,1,0:T(2,128)(2,1)}, u32[]{:S(2)}, u32[]{:S(2)}) %all-to-all-start.3) | async-done | bytes 3670048 | tf_op jit(solution)/shard_map/all_to_all | solution.py:52
  439.7 8.6 %reshape.94 = bf16[1024,1792]{1,0:T(8,128)(2,1)} reshape(bf16[32,16,2,1792]{3,2,1,0:T(2,128)(2,1)} %all-to-all-done.3) | data formatting | bytes 7340032 | tf_op jit(solution)/shard_map/reshape | solution.py:53
  448.3 7.3 %gather_fusion = bf16[512,1792]{1,0:T(8,128)(2,1)} fusion(bf16[1024,1792]{1,0:T(8,128)(2,1)} %reshape.94, s32[1024]{0:T(1024)S(1)} %pad_clamp_fusion), kind=kCustom, calls=%fused_computation | custom fusion | bytes 3672064 | tf_op jit(solution)/shard_map/jit(_take)/gather | solution.py:54
  455.5 0.0 copy-start.1
  455.5 3.2 select_select_fusion
  458.7 0.0 copy-done.1
  (4 shorter events, 0.0 us)
Async XLA Ops:
  0.0 99.8 %copy-start = (bf16[1,512,1792]{2,1,0:T(8,128)(2,1)S(1)}, bf16[1,512,1792]{2,1,0:T(8,128)(2,1)}, u32[]{:S(2)}) copy-start(bf16[1,512,1792]{2,1,0:T(8,128)(2,1)} %param.11) | copy-start | bytes 5505028
  32.1 67.2 %copy-start.2 = (bf16[1,16,16]{2,1,0:T(8,128)(2,1)S(1)}, bf16[1,16,16]{2,1,0:T(8,128)(2,1)}, u32[]{:S(2)}) copy-start(bf16[1,16,16]{2,1,0:T(8,128)(2,1)} %param.10) | copy-start | bytes 1540
  387.1 52.5 %all-to-all-start.3 = ((bf16[32,16,2,1792]{3,2,1,0:T(2,128)(2,1)}), bf16[32,16,2,1792]{3,2,1,0:T(2,128)(2,1)}, u32[]{:S(2)}, u32[]{:S(2)}) async-start(bf16[32,16,2,1792]{3,2,1,0:T(2,128)(2,1)} %bitcast.32), calls=%async_computation.3 | async-start | bytes 7340032 | tf_op jit(solution)/shard_map/all_to_all | solution.py:52
  455.5 3.2 copy-start.1
where the time goes:
time: 464 us; the launch traced here: 459 us
  blocking collectives  261 us (56%)
  local copies, waits for them, and re-layouts  135 us (29%)
  waiting for transfers between devices  47.5 us (10%)
  starting transfers between devices  5.01 us (1%)
    all_to_all x1, blocking collectives, on_device(): lax.all_to_all(result, 'tensor', split_axis=3, concat_axis=1, tiled=True)  170 us
    all_to_all x1, blocking collectives, on_device(): lax.all_to_all(lax.all_to_all(buffer, 'dp', split_axis=0, concat_axis=0,...  66.4 us
    all_to_all x1, waiting for transfers between devices, on_device(): lax.all_to_all(split_back, 'dp', split_axis=0, concat_axis=0, tiled=True)  47.5 us
    reshape x2, local copies, waits for them, and re-layouts, on_device(): result = result.astype(jnp.bfloat16).reshape(group_count, 1, cap, FA * BOUT)  43.3 us
    all_to_all x1, local copies, waits for them, and re-layouts, on_device(): lax.all_to_all(result, 'tensor', split_axis=3, concat_axis=1, tiled=True)  35.1 us
    unnamed x8, local copies, waits for them, and re-layouts  34.9 us
    all_to_all x1, blocking collectives, on_device(): lax.all_to_all(buffer, 'dp', split_axis=0, concat_axis=0, tiled=True)  24.7 us
  transfers between devices with their start and end apart: 1, of which 1 were waited for; matrix products, arithmetic and copies ran while one was open for 0% of the time, Pallas kernels for 0%

commit v1 on v0

--- a/solution.py
+++ b/solution.py
@@ -6,6 +6,29 @@
 FA = 16
 BIN = 512
 BOUT = 1792
+
+
+def split_up(x, dim, size):
+    shape = x.shape
+    pieces = x.reshape(*shape[:dim], size, shape[dim] // size, *shape[dim + 1 :])
+    return jnp.moveaxis(pieces, dim, 0)
+
+
+def in_order(parts, dim):
+    shape = list(parts.shape[1:])
+    shape[dim] *= parts.shape[0]
+    return jnp.moveaxis(parts, 0, dim).reshape(shape)
+
+
+def pairwise_exchange(x, axis, split_dim, concat_dim):
+    length, here = (lax.axis_size(axis), lax.axis_index(axis))
+    blocks = split_up(x, split_dim, length)
+    outs = [blocks[here]]
+    for lap in range(1, length):
+        sent = blocks[here ^ lap]
+        outs.append(lax.ppermute(sent, axis, [(i, i ^ lap) for i in range(length)]))
+    blocks = jnp.stack(outs)[here ^ jnp.arange(length)]
+    return in_order(blocks, concat_dim)
 
 
 def on_device(rows_in, adapter_ids, row_counts, adapter_slot, adapter_a, adapter_b):
@@ -48,7 +71,7 @@
         mixed.reshape(group_count * cap * FA, BIN), adapter_b[0], preferred_element_type=jnp.float32
     )
     result = result.astype(jnp.bfloat16).reshape(group_count, 1, cap, FA * BOUT)
-    split_back = lax.all_to_all(result, "tensor", split_axis=3, concat_axis=1, tiled=True)
+    split_back = pairwise_exchange(result, "tensor", 3, 1)
     returned = lax.all_to_all(split_back, "dp", split_axis=0, concat_axis=0, tiled=True)
     returned = returned.reshape(owner_count * cap, returned.shape[3])
     picked = jnp.take(returned, jnp.where(row_live, slot_index, 0), axis=0)

time: 464 us -> 449 us (0.968)
  the two profiles are of different devices: /device:TPU:32 before, /device:TPU:1 now
where the time goes in v1:
time: 449 us; the launch traced here: 448 us
  starting transfers between devices  190 us (42%)
  waiting for transfers between devices  164 us (37%)
  local copies, waits for them, and re-layouts  58.1 us (13%)
  blocking collectives  27.7 us (6%)
    ppermute x15, starting transfers between devices, pairwise_exchange(): outs.append(lax.ppermute(sent, axis, [(i, i ^ lap) for i in range(length)]))  165 us
    ppermute x15, waiting for transfers between devices, pairwise_exchange(): outs.append(lax.ppermute(sent, axis, [(i, i ^ lap) for i in range(length)]))  74.3 us
    all_to_all x1, waiting for transfers between devices, on_device(): lax.all_to_all(lax.all_to_all(buffer, 'dp', split_axis=0, concat_axis=0,...  45.3 us
    all_to_all x1, waiting for transfers between devices, on_device(): lax.all_to_all(split_back, 'dp', split_axis=0, concat_axis=0, tiled=True)  44.8 us
    all_to_all x1, blocking collectives, on_device(): lax.all_to_all(buffer, 'dp', split_axis=0, concat_axis=0, tiled=True)  27.7 us
    all_to_all x1, starting transfers between devices, on_device(): lax.all_to_all(lax.all_to_all(buffer, 'dp', split_axis=0, concat_axis=0,...  12.9 us
    all_to_all x1, starting transfers between devices, on_device(): lax.all_to_all(split_back, 'dp', split_axis=0, concat_axis=0, tiled=True)  12.4 us
    unnamed x34, local copies, waits for them, and re-layouts  11.2 us
  transfers between devices with their start and end apart: 17, of which 7 were waited for; matrix products, arithmetic and copies ran while one was open for 2% of the time, Pallas kernels for 0%

profile of v1, /device:TPU:1, one launch (start us, length us, event | category | flops | bytes accessed | tf_op | source)
XLA Modules:
  0.0 448.2 jit_solution(6603494177847779742)
XLA Ops:
  2.1 3.2 scatter_custom_fusion
  6.5 27.7 %all_to_all.25 = bf16[32,16,2,512]{3,2,1,0:T(2,128)(2,1)S(1)} all-to-all(bf16[32,16,2,512]{3,2,1,0:T(2,128)(2,1)} %reshape.137), channel_id=1, replica_groups=mesh['dp'=32,'tensor'=16] {'dp'}, dimensions={0} | all-to-all | bytes 2097152 | tf_op jit(solution)/shard_map/all_to_all | solution.py:60
  34.2 2.0 copy.68
  36.2 12.9 %all-to-all-start.1 = ((bf16[32,16,2,512]{3,2,0,1:T(2,128)(2,1)}), bf16[32,16,2,512]{3,2,0,1:T(2,128)(2,1)S(1)}, u32[]{:S(2)}, u32[]{:S(2)}) async-start(bf16[32,16,2,512]{3,2,0,1:T(2,128)(2,1)} %copy.68), calls=%async_computation.1 | async-start | bytes 2097152 | tf_op jit(solution)/shard_map/all_to_all | solution.py:59
  49.3 45.3 %all-to-all-done.1 = bf16[32,16,2,512]{3,2,0,1:T(2,128)(2,1)S(1)} async-done(((bf16[32,16,2,512]{3,2,0,1:T(2,128)(2,1)}), bf16[32,16,2,512]{3,2,0,1:T(2,128)(2,1)S(1)}, u32[]{:S(2)}, u32[]{:S(2)}) %all-to-all-start.1) | async-done | bytes 1048608 | tf_op jit(solution)/shard_map/all_to_all | solution.py:59
  96.0 2.1 convolution_convert_fusion
  98.0 10.8 %constant_dynamic-slice_fusion = (bf16[32,1,2,1,1792]{4,3,2,0,1:T(2,128)(2,1)S(1)}, bf16[32,1,2,1,1792]{4,3,2,0,1:T(2,128)(2,1)S(1)}, bf16[32,1,2,1,1792]{4,3,2,...) fusion(bf16[32,1,2,16,1792]{4,3,2,0,1:T(8,128)(2,1)S(1)} %bitca, ...), kind=kLoop, calls=%fused_computation.55 | loop fusion | bytes 7340096 | tf_op jit(solution)/shard_map/dynamic-slice.15
  109.1 2.9 collective-permute-start
  111.9 5.8 %collective-permute-start.1 = (bf16[32,1,2,1792]{3,0,2,1:T(8,128)(2,1)S(1)}, bf16[32,1,2,1792]{3,0,2,1:T(8,128)(2,1)S(1)}, u32[]{:S(2)}, u32[]{:S(2)}) collective-permute-start(bf16[32,1,2,1792]{3,0,2,1:T(8,128)(2,1)S(1)} %bitcast.132), channel_id=1, source_target_pairs={{0,2},{1,3},{2,0},{3,1},{4,6},{5,7},{6,4},{7,5},{8,10},{9,11},{10,... | collective-permute-start | bytes 688136 | tf_op jit(solution)/shard_map/ppermute | solution.py:29
  119.6 8.9 %collective-permute-start.3 = (bf16[32,1,2,1792]{3,0,2,1:T(8,128)(2,1)S(1)}, bf16[32,1,2,1792]{3,0,2,1:T(8,128)(2,1)S(1)}, u32[]{:S(2)}, u32[]{:S(2)}) collective-permute-start(bf16[32,1,2,1792]{3,0,2,1:T(8,128)(2,1)S(1)} %bitcast.128), channel_id=1, source_target_pairs={{0,4},{1,5},{2,6},{3,7},{4,0},{5,1},{6,2},{7,3},{8,12},{9,13},{10,... | collective-permute-start | bytes 688136 | tf_op jit(solution)/shard_map/ppermute | solution.py:29
  128.5 2.0 collective-permute-start.4
  131.7 9.2 %collective-permute-start.5 = (bf16[32,1,2,1792]{3,0,2,1:T(8,128)(2,1)S(1)}, bf16[32,1,2,1792]{3,0,2,1:T(8,128)(2,1)S(1)}, u32[]{:S(2)}, u32[]{:S(2)}) collective-permute-start(bf16[32,1,2,1792]{3,0,2,1:T(8,128)(2,1)S(1)} %bitcast.133), channel_id=1, source_target_pairs={{0,6},{1,7},{2,4},{3,5},{4,2},{5,3},{6,0},{7,1},{8,14},{9,15},{10,... | collective-permute-start | bytes 688136 | tf_op jit(solution)/shard_map/ppermute | solution.py:29
  141.6 3.6 collective-permute-start.6
  145.9 8.4 %collective-permute-start.7 = (bf16[32,1,2,1792]{3,0,2,1:T(8,128)(2,1)S(1)}, bf16[32,1,2,1792]{3,0,2,1:T(8,128)(2,1)S(1)}, u32[]{:S(2)}, u32[]{:S(2)}) collective-permute-start(bf16[32,1,2,1792]{3,0,2,1:T(8,128)(2,1)S(1)} %bitcast.129), channel_id=1, source_target_pairs={{0,8},{1,9},{2,10},{3,11},{4,12},{5,13},{6,14},{7,15},{8,0},{9,1},... | collective-permute-start | bytes 688136 | tf_op jit(solution)/shard_map/ppermute | solution.py:29
  155.1 21.5 %collective-permute-start.8 = (bf16[32,1,2,1792]{3,0,2,1:T(8,128)(2,1)S(1)}, bf16[32,1,2,1792]{3,0,2,1:T(8,128)(2,1)S(1)}, u32[]{:S(2)}, u32[]{:S(2)}) collective-permute-start(bf16[32,1,2,1792]{3,0,2,1:T(8,128)(2,1)S(1)} %bitcast.127), channel_id=1, source_target_pairs={{0,9},{1,8},{2,11},{3,10},{4,13},{5,12},{6,15},{7,14},{8,1},{9,0},... | collective-permute-start | bytes 688136 | tf_op jit(solution)/shard_map/ppermute | solution.py:29
  177.4 63.7 %collective-permute-start.9 = (bf16[32,1,2,1792]{3,0,2,1:T(8,128)(2,1)S(1)}, bf16[32,1,2,1792]{3,0,2,1:T(8,128)(2,1)S(1)}, u32[]{:S(2)}, u32[]{:S(2)}) collective-permute-start(bf16[32,1,2,1792]{3,0,2,1:T(8,128)(2,1)S(1)} %bitcast.125), channel_id=1, source_target_pairs={{0,10},{1,11},{2,8},{3,9},{4,14},{5,15},{6,12},{7,13},{8,2},{9,3},... | collective-permute-start | bytes 688136 | tf_op jit(solution)/shard_map/ppermute | solution.py:29
  244.4 5.3 %collective-permute-start.11 = (bf16[32,1,2,1792]{3,0,2,1:T(8,128)(2,1)S(1)}, bf16[32,1,2,1792]{3,0,2,1:T(8,128)(2,1)S(1)}, u32[]{:S(2)}, u32[]{:S(2)}) collective-permute-start(bf16[32,1,2,1792]{3,0,2,1:T(8,128)(2,1)S(1)} %bitcast.123), channel_id=1, source_target_pairs={{0,12},{1,13},{2,14},{3,15},{4,8},{5,9},{6,10},{7,11},{8,4},{9,5},... | collective-permute-start | bytes 688136 | tf_op jit(solution)/shard_map/ppermute | solution.py:29
  250.5 3.8 collective-permute-start.12
  255.1 19.2 %collective-permute-start.13 = (bf16[32,1,2,1792]{3,0,2,1:T(8,128)(2,1)S(1)}, bf16[32,1,2,1792]{3,0,2,1:T(8,128)(2,1)S(1)}, u32[]{:S(2)}, u32[]{:S(2)}) collective-permute-start(bf16[32,1,2,1792]{3,0,2,1:T(8,128)(2,1)S(1)} %bitcast.121), channel_id=1, source_target_pairs={{0,14},{1,15},{2,12},{3,13},{4,10},{5,11},{6,8},{7,9},{8,6},{9,7},... | collective-permute-start | bytes 688136 | tf_op jit(solution)/shard_map/ppermute | solution.py:29
  275.0 6.4 %collective-permute-start.14 = (bf16[32,1,2,1792]{3,0,2,1:T(8,128)(2,1)S(1)}, bf16[32,1,2,1792]{3,0,2,1:T(8,128)(2,1)S(1)}, u32[]{:S(2)}, u32[]{:S(2)}) collective-permute-start(bf16[32,1,2,1792]{3,0,2,1:T(8,128)(2,1)S(1)} %bitcast.120), channel_id=1, source_target_pairs={{0,15},{1,14},{2,13},{3,12},{4,11},{5,10},{6,9},{7,8},{8,7},{9,6},... | collective-permute-start | bytes 688136 | tf_op jit(solution)/shard_map/ppermute | solution.py:29
  282.1 52.2 %collective-permute-done.10 = bf16[32,1,2,1792]{3,0,2,1:T(8,128)(2,1)S(1)} collective-permute-done((bf16[32,1,2,1792]{3,0,2,1:T(8,128)(2,1)S(1)}, bf16[32,1,2,1792]{3,0,2,1:T(8,128)(2,1)S(1)}, u32[]{:S(2)}, u32[]{:S(2)}) %collective-permute-start.10) | collective-permute-done | bytes 229408 | tf_op jit(solution)/shard_map/ppermute | solution.py:29
  335.0 4.2 collective-permute-done.11
  339.9 4.2 collective-permute-done.12
  344.8 6.5 %collective-permute-done.13 = bf16[32,1,2,1792]{3,0,2,1:T(8,128)(2,1)S(1)} collective-permute-done((bf16[32,1,2,1792]{3,0,2,1:T(8,128)(2,1)S(1)}, bf16[32,1,2,1792]{3,0,2,1:T(8,128)(2,1)S(1)}, u32[]{:S(2)}, u32[]{:S(2)}) %collective-permute-start.13) | collective-permute-done | bytes 229408 | tf_op jit(solution)/shard_map/ppermute | solution.py:29
  352.1 7.1 %collective-permute-done.14 = bf16[32,1,2,1792]{3,0,2,1:T(8,128)(2,1)S(1)} collective-permute-done((bf16[32,1,2,1792]{3,0,2,1:T(8,128)(2,1)S(1)}, bf16[32,1,2,1792]{3,0,2,1:T(8,128)(2,1)S(1)}, u32[]{:S(2)}, u32[]{:S(2)}) %collective-permute-start.14) | collective-permute-done | bytes 229408 | tf_op jit(solution)/shard_map/ppermute | solution.py:29
  359.9 4.6 %gather_fusion = bf16[16,32,2,1792]{3,1,2,0:T(8,128)(2,1)} fusion(bf16[16,32,2,1792]{3,1,2,0:T(8,128)(2,1)} %bitcast.44, s32[1024]{0:T(1024)S(1)} %pad_clamp_fusion.1), kind=kCustom, calls=%fused_computation | custom fusion | bytes 7340096 | tf_op jit(solution)/shard_map/gather | solution.py:30
  364.5 7.7 %copy.88 = bf16[32,16,2,1792]{3,2,1,0:T(2,128)(2,1)} copy(bf16[32,16,2,1792]{3,0,2,1:T(8,128)(2,1)} %bitcast.116) | data formatting | bytes 7340032 | tf_op jit(solution)/shard_map/reshape | solution.py:20
  372.1 12.4 %all-to-all-start.2 = ((bf16[32,16,2,1792]{3,2,1,0:T(2,128)(2,1)}), bf16[32,16,2,1792]{3,2,1,0:T(2,128)(2,1)}, u32[]{:S(2)}, u32[]{:S(2)}) async-start(bf16[32,16,2,1792]{3,2,1,0:T(2,128)(2,1)} %copy.88), calls=%async_computation.2 | async-start | bytes 7340032 | tf_op jit(solution)/shard_map/all_to_all | solution.py:75
  384.6 44.8 %all-to-all-done.2 = bf16[32,16,2,1792]{3,2,1,0:T(2,128)(2,1)} async-done(((bf16[32,16,2,1792]{3,2,1,0:T(2,128)(2,1)}), bf16[32,16,2,1792]{3,2,1,0:T(2,128)(2,1)}, u32[]{:S(2)}, u32[]{:S(2)}) %all-to-all-start.2) | async-done | bytes 3670048 | tf_op jit(solution)/shard_map/all_to_all | solution.py:75
  429.4 8.6 %reshape.141 = bf16[1024,1792]{1,0:T(8,128)(2,1)} reshape(bf16[32,16,2,1792]{3,2,1,0:T(2,128)(2,1)} %all-to-all-done.2) | data formatting | bytes 7340032 | tf_op jit(solution)/shard_map/reshape | solution.py:76
  438.0 7.3 %gather_fusion.1 = bf16[512,1792]{1,0:T(8,128)(2,1)} fusion(bf16[1024,1792]{1,0:T(8,128)(2,1)} %reshape.141, s32[1024]{0:T(1024)S(1)} %pad_clamp_fusion), kind=kCustom, calls=%fused_computation.1 | custom fusion | bytes 3672064 | tf_op jit(solution)/shard_map/jit(_take)/gather | solution.py:77
  445.2 3.0 select_select_fusion
  (58 shorter events, 19.6 us)
Async XLA Ops:
  0.0 95.9 %copy-start = (bf16[1,512,1792]{2,1,0:T(8,128)(2,1)S(1)}, bf16[1,512,1792]{2,1,0:T(8,128)(2,1)}, u32[]{:S(2)}) copy-start(bf16[1,512,1792]{2,1,0:T(8,128)(2,1)} %param.11) | copy-start | bytes 5505028
  34.2 61.2 %copy-start.1 = (bf16[1,16,16]{2,1,0:T(8,128)(2,1)S(1)}, bf16[1,16,16]{2,1,0:T(8,128)(2,1)}, u32[]{:S(2)}) copy-start(bf16[1,16,16]{2,1,0:T(8,128)(2,1)} %param.10) | copy-start | bytes 1540
  36.2 58.4 %all-to-all-start.1 = ((bf16[32,16,2,512]{3,2,0,1:T(2,128)(2,1)}), bf16[32,16,2,512]{3,2,0,1:T(2,128)(2,1)S(1)}, u32[]{:S(2)}, u32[]{:S(2)}) async-start(bf16[32,16,2,512]{3,2,0,1:T(2,128)(2,1)} %copy.68), calls=%async_computation.1 | async-start | bytes 2097152 | tf_op jit(solution)/shard_map/all_to_all | solution.py:59
  109.1 22.6 %collective-permute-start = (bf16[32,1,2,1792]{3,0,2,1:T(8,128)(2,1)S(1)}, bf16[32,1,2,1792]{3,0,2,1:T(8,128)(2,1)S(1)}, u32[]{:S(2)}, u32[]{:S(2)}) collective-permute-start(bf16[32,1,2,1792]{3,0,2,1:T(8,128)(2,1)S(1)} %bitcast.134), channel_id=1, source_target_pairs={{0,1},{1,0},{2,3},{3,2},{4,5},{5,4},{6,7},{7,6},{8,9},{9,8},{10,11... | collective-permute-start | bytes 688136 | tf_op jit(solution)/shard_map/ppermute | solution.py:29
  111.9 29.7 %collective-permute-start.1 = (bf16[32,1,2,1792]{3,0,2,1:T(8,128)(2,1)S(1)}, bf16[32,1,2,1792]{3,0,2,1:T(8,128)(2,1)S(1)}, u32[]{:S(2)}, u32[]{:S(2)}) collective-permute-start(bf16[32,1,2,1792]{3,0,2,1:T(8,128)(2,1)S(1)} %bitcast.132), channel_id=1, source_target_pairs={{0,2},{1,3},{2,0},{3,1},{4,6},{5,7},{6,4},{7,5},{8,10},{9,11},{10,... | collective-permute-start | bytes 688136 | tf_op jit(solution)/shard_map/ppermute | solution.py:29
  117.7 28.2 %collective-permute-start.2 = (bf16[32,1,2,1792]{3,0,2,1:T(8,128)(2,1)S(1)}, bf16[32,1,2,1792]{3,0,2,1:T(8,128)(2,1)S(1)}, u32[]{:S(2)}, u32[]{:S(2)}) collective-permute-start(bf16[32,1,2,1792]{3,0,2,1:T(8,128)(2,1)S(1)} %bitcast.130), channel_id=1, source_target_pairs={{0,3},{1,2},{2,1},{3,0},{4,7},{5,6},{6,5},{7,4},{8,11},{9,10},{10,... | collective-permute-start | bytes 688136 | tf_op jit(solution)/shard_map/ppermute | solution.py:29
  119.6 35.5 %collective-permute-start.3 = (bf16[32,1,2,1792]{3,0,2,1:T(8,128)(2,1)S(1)}, bf16[32,1,2,1792]{3,0,2,1:T(8,128)(2,1)S(1)}, u32[]{:S(2)}, u32[]{:S(2)}) collective-permute-start(bf16[32,1,2,1792]{3,0,2,1:T(8,128)(2,1)S(1)} %bitcast.128), channel_id=1, source_target_pairs={{0,4},{1,5},{2,6},{3,7},{4,0},{5,1},{6,2},{7,3},{8,12},{9,13},{10,... | collective-permute-start | bytes 688136 | tf_op jit(solution)/shard_map/ppermute | solution.py:29
  128.5 48.8 %collective-permute-start.4 = (bf16[32,1,2,1792]{3,0,2,1:T(8,128)(2,1)S(1)}, bf16[32,1,2,1792]{3,0,2,1:T(8,128)(2,1)S(1)}, u32[]{:S(2)}, u32[]{:S(2)}) collective-permute-start(bf16[32,1,2,1792]{3,0,2,1:T(8,128)(2,1)S(1)} %bitcast.126), channel_id=1, source_target_pairs={{0,5},{1,4},{2,7},{3,6},{4,1},{5,0},{6,3},{7,2},{8,13},{9,12},{10,... | collective-permute-start | bytes 688136 | tf_op jit(solution)/shard_map/ppermute | solution.py:29
  131.7 110.1 %collective-permute-start.5 = (bf16[32,1,2,1792]{3,0,2,1:T(8,128)(2,1)S(1)}, bf16[32,1,2,1792]{3,0,2,1:T(8,128)(2,1)S(1)}, u32[]{:S(2)}, u32[]{:S(2)}) collective-permute-start(bf16[32,1,2,1792]{3,0,2,1:T(8,128)(2,1)S(1)} %bitcast.133), channel_id=1, source_target_pairs={{0,6},{1,7},{2,4},{3,5},{4,2},{5,3},{6,0},{7,1},{8,14},{9,15},{10,... | collective-permute-start | bytes 688136 | tf_op jit(solution)/shard_map/ppermute | solution.py:29
  141.6 102.8 %collective-permute-start.6 = (bf16[32,1,2,1792]{3,0,2,1:T(8,128)(2,1)S(1)}, bf16[32,1,2,1792]{3,0,2,1:T(8,128)(2,1)S(1)}, u32[]{:S(2)}, u32[]{:S(2)}) collective-permute-start(bf16[32,1,2,1792]{3,0,2,1:T(8,128)(2,1)S(1)} %bitcast.131), channel_id=1, source_target_pairs={{0,7},{1,6},{2,5},{3,4},{4,3},{5,2},{6,1},{7,0},{8,15},{9,14},{10,... | collective-permute-start | bytes 688136 | tf_op jit(solution)/shard_map/ppermute | solution.py:29
  145.9 104.6 %collective-permute-start.7 = (bf16[32,1,2,1792]{3,0,2,1:T(8,128)(2,1)S(1)}, bf16[32,1,2,1792]{3,0,2,1:T(8,128)(2,1)S(1)}, u32[]{:S(2)}, u32[]{:S(2)}) collective-permute-start(bf16[32,1,2,1792]{3,0,2,1:T(8,128)(2,1)S(1)} %bitcast.129), channel_id=1, source_target_pairs={{0,8},{1,9},{2,10},{3,11},{4,12},{5,13},{6,14},{7,15},{8,0},{9,1},... | collective-permute-start | bytes 688136 | tf_op jit(solution)/shard_map/ppermute | solution.py:29
  155.1 100.0 %collective-permute-start.8 = (bf16[32,1,2,1792]{3,0,2,1:T(8,128)(2,1)S(1)}, bf16[32,1,2,1792]{3,0,2,1:T(8,128)(2,1)S(1)}, u32[]{:S(2)}, u32[]{:S(2)}) collective-permute-start(bf16[32,1,2,1792]{3,0,2,1:T(8,128)(2,1)S(1)} %bitcast.127), channel_id=1, source_target_pairs={{0,9},{1,8},{2,11},{3,10},{4,13},{5,12},{6,15},{7,14},{8,1},{9,0},... | collective-permute-start | bytes 688136 | tf_op jit(solution)/shard_map/ppermute | solution.py:29
  177.4 97.7 %collective-permute-start.9 = (bf16[32,1,2,1792]{3,0,2,1:T(8,128)(2,1)S(1)}, bf16[32,1,2,1792]{3,0,2,1:T(8,128)(2,1)S(1)}, u32[]{:S(2)}, u32[]{:S(2)}) collective-permute-start(bf16[32,1,2,1792]{3,0,2,1:T(8,128)(2,1)S(1)} %bitcast.125), channel_id=1, source_target_pairs={{0,10},{1,11},{2,8},{3,9},{4,14},{5,15},{6,12},{7,13},{8,2},{9,3},... | collective-permute-start | bytes 688136 | tf_op jit(solution)/shard_map/ppermute | solution.py:29
  241.8 92.5 %collective-permute-start.10 = (bf16[32,1,2,1792]{3,0,2,1:T(8,128)(2,1)S(1)}, bf16[32,1,2,1792]{3,0,2,1:T(8,128)(2,1)S(1)}, u32[]{:S(2)}, u32[]{:S(2)}) collective-permute-start(bf16[32,1,2,1792]{3,0,2,1:T(8,128)(2,1)S(1)} %bitcast.124), channel_id=1, source_target_pairs={{0,11},{1,10},{2,9},{3,8},{4,15},{5,14},{6,13},{7,12},{8,3},{9,2},... | collective-permute-start | bytes 688136 | tf_op jit(solution)/shard_map/ppermute | solution.py:29
  244.4 94.8 %collective-permute-start.11 = (bf16[32,1,2,1792]{3,0,2,1:T(8,128)(2,1)S(1)}, bf16[32,1,2,1792]{3,0,2,1:T(8,128)(2,1)S(1)}, u32[]{:S(2)}, u32[]{:S(2)}) collective-permute-start(bf16[32,1,2,1792]{3,0,2,1:T(8,128)(2,1)S(1)} %bitcast.123), channel_id=1, source_target_pairs={{0,12},{1,13},{2,14},{3,15},{4,8},{5,9},{6,10},{7,11},{8,4},{9,5},... | collective-permute-start | bytes 688136 | tf_op jit(solution)/shard_map/ppermute | solution.py:29
  250.5 93.6 %collective-permute-start.12 = (bf16[32,1,2,1792]{3,0,2,1:T(8,128)(2,1)S(1)}, bf16[32,1,2,1792]{3,0,2,1:T(8,128)(2,1)S(1)}, u32[]{:S(2)}, u32[]{:S(2)}) collective-permute-start(bf16[32,1,2,1792]{3,0,2,1:T(8,128)(2,1)S(1)} %bitcast.122), channel_id=1, source_target_pairs={{0,13},{1,12},{2,15},{3,14},{4,9},{5,8},{6,11},{7,10},{8,5},{9,4},... | collective-permute-start | bytes 688136 | tf_op jit(solution)/shard_map/ppermute | solution.py:29
  255.1 96.3 %collective-permute-start.13 = (bf16[32,1,2,1792]{3,0,2,1:T(8,128)(2,1)S(1)}, bf16[32,1,2,1792]{3,0,2,1:T(8,128)(2,1)S(1)}, u32[]{:S(2)}, u32[]{:S(2)}) collective-permute-start(bf16[32,1,2,1792]{3,0,2,1:T(8,128)(2,1)S(1)} %bitcast.121), channel_id=1, source_target_pairs={{0,14},{1,15},{2,12},{3,13},{4,10},{5,11},{6,8},{7,9},{8,6},{9,7},... | collective-permute-start | bytes 688136 | tf_op jit(solution)/shard_map/ppermute | solution.py:29
  275.0 84.1 %collective-permute-start.14 = (bf16[32,1,2,1792]{3,0,2,1:T(8,128)(2,1)S(1)}, bf16[32,1,2,1792]{3,0,2,1:T(8,128)(2,1)S(1)}, u32[]{:S(2)}, u32[]{:S(2)}) collective-permute-start(bf16[32,1,2,1792]{3,0,2,1:T(8,128)(2,1)S(1)} %bitcast.120), channel_id=1, source_target_pairs={{0,15},{1,14},{2,13},{3,12},{4,11},{5,10},{6,9},{7,8},{8,7},{9,6},... | collective-permute-start | bytes 688136 | tf_op jit(solution)/shard_map/ppermute | solution.py:29
  372.1 57.2 %all-to-all-start.2 = ((bf16[32,16,2,1792]{3,2,1,0:T(2,128)(2,1)}), bf16[32,16,2,1792]{3,2,1,0:T(2,128)(2,1)}, u32[]{:S(2)}, u32[]{:S(2)}) async-start(bf16[32,16,2,1792]{3,2,1,0:T(2,128)(2,1)} %copy.88), calls=%async_computation.2 | async-start | bytes 7340032 | tf_op jit(solution)/shard_map/all_to_all | solution.py:75
